TPU v7x, 32 devices: a whole 2x2x4 slice. The times are simulated.
32 devices in a mesh: win: 2 (over x), wide: 8 (over z, y), narrow: 2 (over core).
Axes of the slice: x: 2, y: 2, z: 4, core: 2. Of those that a mesh axis runs over, the one named last changes fastest.
Arguments:
- window_data: float32 [384, 128, 256], P(('win', 'wide'), 'narrow'), parts along dimension 0, may hold values from -6 to 6
- factor_one: float32 [256, 48], P(('win', 'narrow')), parts along dimension 0, may hold values from -0.5 to 0.5
- factor_two: float32 [512, 48], P('win'), parts along dimension 0, may hold values from -0.375 to 0.375
- factor_three: float32 [384, 48], P(('win', 'wide')), parts along dimension 0, may hold values from -0.4375 to 0.4375
Outputs:
- basis_one: float32 [256, 48], P(('win', 'narrow')), parts along dimension 0
- basis_two: float32 [512, 48], P('win'), parts along dimension 0
- basis_three: float32 [384, 48], P(('win', 'wide')), parts along dimension 0
- core_unfolded: float32 [48, 4608], P(None, ('win', 'wide', 'narrow')), parts along dimension 1
There are 2 independent parts, one for each index of `win`. A program takes and returns all parts, laid end to end along the dimension named above; each array names one. Nothing has to cross between parts.
All inputs are finite; a program needn't handle non-finite values.
Results may differ from a plain program's by a relative error of at most 0.0003.
Values sent between devices are 32-bit elements; how exact they have to be, the bound alone decides.
A program may use at most 64 MiB of HBM per device.

v0:
```python
import jax
import jax.numpy as jnp
from jax import lax
from jax.sharding import PartitionSpec as P

highest = lax.Precision.HIGHEST


def contract(form, left, right):
    return jnp.einsum(form, left, right, precision=highest)


def orthonormal(basis, gram):
    lower = jnp.linalg.cholesky(gram)
    return lax.linalg.triangular_solve(lower, basis, left_side=False, lower=True, transpose_a=True)


def full_core(partial_value):
    flat = partial_value.reshape(
        partial_value.shape[0], partial_value.shape[1] * partial_value.shape[2]
    )
    shares = lax.psum_scatter(flat, ("wide", "narrow"), scatter_dimension=1, tiled=True)
    whole = lax.all_gather(shares, ("wide", "narrow"), axis=1, tiled=True)
    return whole.reshape(partial_value.shape)


def on_device(window_data, factor_one, factor_two, factor_three):
    rank = factor_one.shape[1]
    along_two = contract("kij,jb->kib", window_data, factor_two)
    unfold_part = contract("kib,kc->ibc", along_two, factor_three).reshape(
        along_two.shape[1], rank * rank
    )
    unfold_rows = lax.psum_scatter(unfold_part, "wide", scatter_dimension=1, tiled=True)
    weights_one = lax.psum(jnp.dot(unfold_rows.T, factor_one, precision=highest), "narrow")
    product_one = lax.psum(jnp.dot(unfold_rows, weights_one, precision=highest), "wide")
    gram_one = lax.psum(jnp.dot(product_one.T, product_one, precision=highest), "narrow")
    basis_one = orthonormal(product_one, gram_one)
    along_one = contract("kij,ia->kaj", window_data, basis_one)
    core_two = full_core(
        contract("kab,kc->abc", contract("kaj,jb->kab", along_one, factor_two), factor_three)
    )
    spread_two = contract("abc,kc->kab", core_two, factor_three)
    product_two = lax.psum(contract("kaj,kab->jb", along_one, spread_two), ("wide", "narrow"))
    basis_two = orthonormal(product_two, jnp.dot(product_two.T, product_two, precision=highest))
    along_new = contract("kij,jb->kib", window_data, basis_two)
    unfold_three = contract("kib,ia->kab", along_new, basis_one)
    core_three = full_core(contract("kab,kc->abc", unfold_three, factor_three))
    product_three = lax.psum(contract("kab,abc->kc", unfold_three, core_three), "narrow")
    gram_three = lax.psum(jnp.dot(product_three.T, product_three, precision=highest), "wide")
    basis_three = orthonormal(product_three, gram_three)
    core_part = contract("kab,kc->abc", unfold_three, basis_three).reshape(rank, rank * rank)
    core_shares = lax.psum_scatter(core_part, ("wide", "narrow"), scatter_dimension=1, tiled=True)
    return (basis_one, basis_two, basis_three, core_shares)


def solution(mesh):
    return jax.shard_map(
        on_device,
        mesh=mesh,
        in_specs=(
            P(("win", "wide"), "narrow", None),
            P(("win", "narrow"), None),
            P("win", None),
            P(("win", "wide"), None),
        ),
        out_specs=(
            P(("win", "narrow"), None),
            P("win", None),
            P(("win", "wide"), None),
            P(None, ("win", "wide", "narrow")),
        ),
        check_vma=False,
    )
```

profile of v0, /device:TPU:0, one launch (start us, length us, event | category | flops | bytes accessed | tf_op | source)
XLA Modules:
  0.0 504.9 jit_solution(5925950153966513324)
XLA Ops:
  8.6 3.1 fusion.12
  13.9 67.2 %reduce-scatter.11.cloned.1.call-done = f32[64,288]{0,1:T(8,128)} async-done(((f32[64,2304]{0,1:T(8,128)}), f32[64,288]{0,1:T(8,128)}) %reduce-scatter.11.cloned.1.call-update) | async-done | bytes 73744 | tf_op jit(solution)/shard_map/reduce_scatter | solution.py:33
  82.4 3.5 psum.42
  87.0 35.2 %psum.43 = f32[64,48]{0,1:T(8,128)S(1)} all-reduce(f32[64,48]{0,1:T(8,128)S(1)} %fusion.35), channel_id=1, replica_groups=mesh['win'=2,'wide'=8,'narrow'=2] {'wide'}, use_global_device_ids=true, to_apply=%region_2.0 | all-reduce | flops 3072 | bytes 24576 | tf_op jit(solution)/shard_map/psum | solution.py:35
  122.4 3.4 psum.44
  125.9 4.4 cholesky.59
  131.6 3.7 custom-call.11
  138.3 3.1 fusion.31
  141.4 2.7 copy.45
  144.2 55.4 %reduce-scatter.13.cloned.1.call-done = f32[144,48]{1,0:T(8,128)} async-done(((f32[2304,48]{1,0:T(8,128)}), f32[144,48]{1,0:T(8,128)}) %reduce-scatter.13.cloned.1.call-update) | async-done | bytes 27664
  200.6 21.8 %all-gather = f32[16,144,48]{1,2,0:T(8,128)S(1)} all-gather(f32[1,144,48]{1,2,0:T(8,128)S(1)} %bitcast.116), channel_id=1, replica_groups=mesh['win'=2,'wide'=8,'narrow'=2] {'wide','narrow'}, dimensions={0}, use_global_device_ids=true | all-gather | bytes 470016 | tf_op jit(solution)/shard_map/all_gather | solution.py:23
  224.0 2.7 reshape.42
  226.7 4.7 convolution_bitcast_fusion.3
  232.6 57.9 %psum.45 = f32[256,48]{0,1:T(8,128)S(1)} all-reduce(f32[256,48]{0,1:T(8,128)S(1)} %convolution_bitcast_fusion.4), channel_id=1, replica_groups=mesh['win'=2,'wide'=8,'narrow'=2] {'wide','narrow'}, use_global_device_ids=true, to_apply=%region_7.0 | all-reduce | flops 12288 | bytes 98304 | tf_op jit(solution)/shard_map/psum | solution.py:43
  290.8 4.4 cholesky.70
  296.5 3.7 custom-call.12
  300.5 2.3 convolution_bitcast_fusion.2
  308.6 55.5 %reduce-scatter.15.cloned.1.call-done = f32[144,48]{1,0:T(8,128)} async-done(((f32[2304,48]{1,0:T(8,128)}), f32[144,48]{1,0:T(8,128)}) %reduce-scatter.15.cloned.1.call-update) | async-done | bytes 27664
  365.0 21.8 %all-gather.1 = f32[16,144,48]{1,2,0:T(8,128)S(1)} all-gather(f32[1,144,48]{1,2,0:T(8,128)S(1)} %bitcast.117), channel_id=1, replica_groups=mesh['win'=2,'wide'=8,'narrow'=2] {'wide','narrow'}, dimensions={0}, use_global_device_ids=true | all-gather | bytes 470016 | tf_op jit(solution)/shard_map/all_gather | solution.py:23
  391.4 3.5 psum.46
  395.1 33.0 %psum.47 = f32[48,48]{0,1:T(8,128)S(1)} all-reduce(f32[48,48]{0,1:T(8,128)S(1)} %fusion.38), channel_id=1, replica_groups=mesh['win'=2,'wide'=8,'narrow'=2] {'wide'}, use_global_device_ids=true, to_apply=%region_10.12 | all-reduce | flops 2304 | bytes 18432 | tf_op jit(solution)/shard_map/psum | solution.py:49
  428.2 4.4 cholesky.81
  433.9 3.7 custom-call.13
  441.4 55.4 %reduce-scatter.17.cloned.1.call-done = f32[144,48]{1,0:T(8,128)} async-done(((f32[2304,48]{1,0:T(8,128)}), f32[144,48]{1,0:T(8,128)}) %reduce-scatter.17.cloned.1.call-update) | async-done | bytes 27664
  (65 shorter events, 34.3 us)
Async XLA Ops:
  7.2 1.4 copy-start
  7.2 4.5 copy-start.3
  7.2 74.0 %reduce-scatter.11.cloned.1.call-start = ((), (), s32[]{:S(2)}) async-start(), calls=%async_computation.4 | async-start | bytes 1327104 | tf_op jit(solution)/shard_map/reduce_scatter | solution.py:33
  11.7 69.5 %copy-start.7 = (f32[64,48]{0,1:T(8,128)S(1)}, f32[64,48]{0,1:T(8,128)}, u32[]{:S(2)}) copy-start(f32[64,48]{0,1:T(8,128)} %param.6) | copy-start | bytes 36868
  13.9 185.7 %reduce-scatter.13.cloned.1.call-start = ((), (), s32[]{:S(2)}) async-start(), calls=%async_computation.5 | async-start | bytes 1253376
  135.5 1.1 copy-start.1
  135.5 1.1 copy-start.5
  144.1 219.9 %reduce-scatter.15.cloned.1.call-start = ((), (), s32[]{:S(2)}) async-start(), calls=%async_computation.6 | async-start | bytes 1253376
  296.5 6.3 %copy-start.2 = (f32[64,48]{0,1:T(8,128)S(1)}, f32[64,48]{0,1:T(8,128)}, u32[]{:S(2)}) copy-start(f32[64,48]{0,1:T(8,128)} %copy-done.1) | copy-start | bytes 36868
  300.5 4.5 copy-start.4
  308.5 188.3 %reduce-scatter.17.cloned.1.call-start = ((), (), s32[]{:S(2)}) async-start(), calls=%async_computation.7 | async-start | bytes 1253376
  437.8 3.6 copy-start.6
Sparse Core Ops, SparseCore 0:
  14.0 67.1 reduce-scatter.10
  144.2 55.3 reduce-scatter.12
  308.7 55.3 reduce-scatter.14
  441.5 55.2 reduce-scatter.16
where the time goes:
time: 506 us; the launch traced here: 505 us
  waiting for transfers between devices  234 us (46%)
  blocking collectives  180 us (36%)
  matrix products  30.3 us (6%)
  other arithmetic  28.2 us (6%)
  local copies, waits for them, and re-layouts  18.5 us (4%)
  between operations  14.1 us (3%)
    unnamed x7, waiting for transfers between devices  166 us
    reduce_scatter x1, waiting for transfers between devices, on_device(): lax.psum_scatter(unfold_part, 'wide', scatter_dimension=1, tiled=True)  67.2 us
    psum x1, blocking collectives, on_device(): lax.psum(contract('kaj,kab->jb', along_one, spread_two), ('wide', 'narrow'))  57.9 us
    all_gather x2, blocking collectives, full_core(): whole = lax.all_gather(shares, ('wide', 'narrow'), axis=1, tiled=True)  43.6 us
    psum x1, blocking collectives, on_device(): lax.psum(jnp.dot(unfold_rows, weights_one, precision=highest), 'wide')  35.2 us
    psum x1, blocking collectives, on_device(): lax.psum(jnp.dot(product_three.T, product_three, precision=highest), 'wide')  33 us
    dot_general x12, matrix products, contract(): return jnp.einsum(form, left, right, precision=highest)  26.7 us
    another operation x9, other arithmetic, orthonormal(): lower = jnp.linalg.cholesky(gram)  15.2 us
  transfers between devices with their start and end apart: 4, of which 4 were waited for; matrix products, arithmetic and copies ran while one was open for 0% of the time, Pallas kernels for 0%

commit v1 on v0

--- a/solution.py
+++ b/solution.py
@@ -1,13 +1,294 @@
+import functools
+
 import jax
 import jax.numpy as jnp
 from jax import lax
+from jax.experimental import pallas as pl
+from jax.experimental.pallas import tpu as pltpu
 from jax.sharding import PartitionSpec as P
 
 highest = lax.Precision.HIGHEST
+vmem = pl.BlockSpec(memory_space=pltpu.VMEM)
 
 
 def contract(form, left, right):
     return jnp.einsum(form, left, right, precision=highest)
+
+
+def dot(left, right):
+    return jnp.dot(left, right, precision=highest, preferred_element_type=jnp.float32)
+
+
+def dot_t(left, right):
+    return lax.dot_general(
+        left, right, (((0,), (0,)), ((), ())), precision=highest, preferred_element_type=jnp.float32
+    )
+
+
+def dot_rt(left, right):
+    return lax.dot_general(
+        left, right, (((1,), (1,)), ((), ())), precision=highest, preferred_element_type=jnp.float32
+    )
+
+
+def inverse_lower(gram):
+    rank = gram.shape[0]
+    group = 8
+    rows = lax.broadcasted_iota(jnp.int32, (rank, rank), 0)
+    columns = lax.broadcasted_iota(jnp.int32, (rank, rank), 1)
+    both = jnp.concatenate([gram, (rows == columns).astype(jnp.float32)], axis=1)
+    blocks = [both[at : at + group] for at in range(0, rank, group)]
+    inside = lax.broadcasted_iota(jnp.int32, (group, 2 * rank), 0)
+    scales = []
+    for step in range(rank):
+        at, row = divmod(step, group)
+        pivot_row = blocks[at][row : row + 1]
+        pivot = pivot_row[:, step : step + 1]
+        scales.append(lax.rsqrt(pivot))
+        scaled = pivot_row * (1.0 / pivot)
+        for later in range(at, rank // group):
+            change = blocks[later][:, step : step + 1] * scaled
+            if later == at:
+                change = jnp.where(inside > row, change, 0.0)
+            blocks[later] = blocks[later] - change
+    right = jnp.concatenate(blocks, axis=0)[:, rank:]
+    return right * jnp.concatenate(scales, axis=0)
+
+
+class Link:
+    def __init__(self, wide, narrow, send, recv):
+        self.wide, self.narrow = wide, narrow
+        self.send, self.recv = send, recv
+        self.used = 0
+        self.started = []
+        self.w = lax.axis_index("wide")
+        self.n = lax.axis_index("narrow")
+
+    def others(self):
+        for step in range(1, self.wide * self.narrow):
+            dw, dn = divmod(step, self.narrow)
+            yield lax.rem(self.w + dw, self.wide), lax.rem(self.n + dn, self.narrow)
+
+    def greet(self):
+        barrier = pltpu.get_barrier_semaphore()
+        for w, n in self.others():
+            pl.semaphore_signal(
+                barrier, inc=1, device_id={"wide": w, "narrow": n}, device_id_type=pl.DeviceIdType.MESH
+            )
+        pl.semaphore_wait(barrier, self.wide * self.narrow - 1)
+
+    def put(self, source, target, w, n):
+        copy = pltpu.make_async_remote_copy(
+            src_ref=source,
+            dst_ref=target,
+            send_sem=self.send.at[self.used],
+            recv_sem=self.recv.at[self.used],
+            device_id={"wide": w, "narrow": n},
+            device_id_type=pl.DeviceIdType.MESH,
+        )
+        self.used += 1
+        copy.start()
+        self.started.append(copy)
+        return copy
+
+    def along_wide(self):
+        return [(step, lax.rem(self.w + step, self.wide)) for step in range(1, self.wide)]
+
+    def close(self):
+        for copy in self.started:
+            copy.wait_send()
+
+
+def mode_one_kernel(wide, narrow, u_ref, f_ref, basis_ref, core_ref,
+                    parts, total, w_send, w_recv, p_send, p_recv, p_all, c_part, c_recv, c_all, send, recv):
+    link = Link(wide, narrow, send, recv)
+    share = total.shape[1]
+    rows = f_ref.shape[0]
+    rank = f_ref.shape[1]
+    per = rank // wide
+    chunk = rows // wide
+    half = rank // narrow
+    link.greet()
+    partner = lax.rem(link.n + 1, narrow)
+    copies = []
+    for step, w in link.along_wide():
+        columns = pl.ds(pl.multiple_of(w * share, 128), share)
+        copies.append(link.put(u_ref.at[:, columns], parts.at[step - 1], w, link.n))
+    added = u_ref[:, pl.ds(pl.multiple_of(link.w * share, 128), share)]
+    for step, copy in enumerate(copies):
+        copy.wait_recv()
+        added = added + parts[step]
+    total[...] = added
+    factor = f_ref[...]
+    for v in range(per):
+        w_send[v] = dot(total[:, v * rows : (v + 1) * rows], factor)
+    copy = link.put(w_send, w_recv, link.w, partner)
+    copy.wait_recv()
+    product = jnp.zeros((rows, rank), jnp.float32)
+    for v in range(per):
+        product = product + dot_t(total[:, v * rows : (v + 1) * rows], w_send[v] + w_recv[v])
+    for w in range(wide):
+        p_send[w] = product[w * chunk : (w + 1) * chunk]
+    copies = [link.put(p_send.at[w], p_recv.at[step - 1], w, link.n) for step, w in link.along_wide()]
+    added = p_send[link.w]
+    for step, copy in enumerate(copies):
+        copy.wait_recv()
+        added = added + p_recv[step]
+    mine = link.n * wide + link.w
+    p_all[mine] = added
+    copies = [link.put(p_all.at[mine], p_all.at[mine], w, n) for w, n in link.others()]
+    for copy in copies:
+        copy.wait_recv()
+    whole = p_all[...].reshape(narrow * rows, rank)
+    inverse = inverse_lower(dot_t(whole, whole))
+    basis = dot_rt(p_all[pl.ds(link.n * wide, wide)].reshape(rows, rank), inverse)
+    basis_ref[...] = basis
+    for v in range(per):
+        c_part[:, v * rank : (v + 1) * rank] = dot(total[:, v * rows : (v + 1) * rows], basis)
+    theirs = pl.ds(pl.multiple_of(partner * half, 8), half)
+    copy = link.put(c_part.at[theirs, :], c_recv, link.w, partner)
+    own = c_part[pl.ds(pl.multiple_of(link.n * half, 8), half), :]
+    copy.wait_recv()
+    c_all[link.w, link.n] = own + c_recv[...]
+    block = c_all.at[link.w, link.n]
+    copies = [link.put(block, block, w, link.n) for _, w in link.along_wide()]
+    passed = [link.put(block, block, link.w, partner)]
+    for (step, _), copy in zip(link.along_wide(), copies):
+        copy.wait_recv()
+        source = lax.rem(link.w + wide - step, wide)
+        block = c_all.at[source, link.n]
+        passed.append(link.put(block, block, link.w, partner))
+    for copy in passed:
+        copy.wait_recv()
+    for w in range(wide):
+        for n in range(narrow):
+            core_ref[w, n * half : (n + 1) * half] = c_all[w, n]
+    link.close()
+
+
+def mode_two_kernel(wide, narrow, p_ref, basis_ref, p_recv, p_all, send, recv):
+    link = Link(wide, narrow, send, recv)
+    group = wide * narrow
+    link.greet()
+    copies = [
+        link.put(p_ref.at[w * narrow + n], p_recv.at[step], w, n)
+        for step, (w, n) in enumerate(link.others())
+    ]
+    mine = link.w * narrow + link.n
+    added = p_ref[mine]
+    for step, copy in enumerate(copies):
+        copy.wait_recv()
+        added = added + p_recv[step]
+    p_all[mine] = added
+    copies = [link.put(p_all.at[mine], p_all.at[mine], w, n) for w, n in link.others()]
+    for copy in copies:
+        copy.wait_recv()
+    whole = p_all[...].reshape(basis_ref.shape)
+    basis_ref[...] = dot_rt(whole, inverse_lower(dot_t(whole, whole)))
+    link.close()
+
+
+def mode_three_kernel(wide, narrow, u_ref, basis_ref, core_ref, u_all, p_send, p_recv, p_all, send, recv):
+    link = Link(wide, narrow, send, recv)
+    group = wide * narrow
+    rows, rank = basis_ref.shape
+    share = core_ref.shape[0]
+    link.greet()
+    copies = [
+        link.put(u_ref.at[w * narrow + n], u_all.at[link.n, link.w], w, n) for w, n in link.others()
+    ]
+    u_all[link.n, link.w] = u_ref[link.w * narrow + link.n]
+    for copy in copies:
+        copy.wait_recv()
+    factor = u_all[0, :, :, share:].reshape(wide * rows, rank)
+    unfold = u_all[0, :, :, :share]
+    for n in range(1, narrow):
+        unfold = unfold + u_all[n, :, :, :share]
+    unfold = unfold.reshape(wide * rows, share)
+    product = dot(unfold, dot_t(unfold, factor))
+    p_send[...] = product.reshape(wide, rows, rank)
+    copies = [link.put(p_send.at[w], p_recv.at[step - 1], w, link.n) for step, w in link.along_wide()]
+    added = p_send[link.w]
+    for step, copy in enumerate(copies):
+        copy.wait_recv()
+        added = added + p_recv[step]
+    p_all[link.n, link.w] = added
+    block = p_all.at[link.n, link.w]
+    copies = [link.put(block, block, w, n) for w, n in link.others()]
+    for copy in copies:
+        copy.wait_recv()
+    whole = p_all[0]
+    for n in range(1, narrow):
+        whole = whole + p_all[n]
+    p_recv[...] = whole
+    whole = whole.reshape(wide * rows, rank)
+    inverse = inverse_lower(dot_t(whole, whole))
+    basis_ref[...] = dot_rt(p_recv[link.w], inverse)
+    core_ref[...] = dot_t(unfold, dot_rt(whole, inverse))
+    link.close()
+
+
+def call(kernel, wide, narrow, outs, scratch, copies, at, operands):
+    return pl.pallas_call(
+        functools.partial(kernel, wide, narrow),
+        out_shape=[jax.ShapeDtypeStruct(shape, jnp.float32) for shape in outs],
+        in_specs=[vmem] * len(operands),
+        out_specs=[vmem] * len(outs),
+        scratch_shapes=[pltpu.VMEM(shape, jnp.float32) for shape in scratch]
+        + [pltpu.SemaphoreType.DMA((copies,))] * 2,
+        compiler_params=pltpu.CompilerParams(
+            collective_id=at, has_side_effects=True, vmem_limit_bytes=32 * 1024 * 1024
+        ),
+    )(*operands)
+
+
+def on_device(wide, narrow, window_data, factor_one, factor_two, factor_three):
+    layers, rows, cells = window_data.shape
+    rank = factor_one.shape[1]
+    group = wide * narrow
+    per = rank // wide
+    share = per * rows
+    along_two = contract("kij,jb->kbi", window_data, factor_two).reshape(layers, rank * rows)
+    unfold_one = contract("kc,kn->cn", factor_three, along_two)
+    basis_one, core_two = call(
+        mode_one_kernel, wide, narrow,
+        [(rows, rank), (wide, rank, per * rank)],
+        [
+            (wide - 1, rank, share), (rank, share),
+            (per, rank, rank), (per, rank, rank),
+            (wide, rows // wide, rank), (wide - 1, rows // wide, rank), (group, rows // wide, rank),
+            (rank, per * rank), (rank // narrow, per * rank), (wide, narrow, rank // narrow, per * rank),
+        ],
+        4 * (wide - 1) + 3 + group - 1, 0, (unfold_one, factor_one),
+    )
+    core_two = core_two.reshape(wide, rank, per, rank)
+    along_one = contract("kij,ia->kaj", window_data, basis_one)
+    spread_two = contract("wcva,kc->kawv", core_two, factor_three).reshape(layers, rank, rank)
+    product_two = contract("kaj,kab->jb", along_one, spread_two)
+    basis_two, = call(
+        mode_two_kernel, wide, narrow,
+        [(cells, rank)],
+        [(group - 1, cells // group, rank), (group, cells // group, rank)],
+        2 * (group - 1), 1, (product_two.reshape(group, cells // group, rank),),
+    )
+    along_new = contract("kij,jb->kib", window_data, basis_two)
+    unfold_three = contract("kib,ia->kba", along_new, basis_one)
+    shares = rank // group * rank
+    unfold_three = unfold_three.reshape(layers, group, shares)
+    unfold_three = jnp.concatenate(
+        [unfold_three, jnp.broadcast_to(factor_three[:, None], (layers, group, rank))], axis=2
+    ).transpose(1, 0, 2)
+    basis_three, core = call(
+        mode_three_kernel, wide, narrow,
+        [(layers, rank), (shares, rank)],
+        [
+            (narrow, wide, layers, shares + rank),
+            (wide, layers, rank), (wide, layers, rank), (narrow, wide, layers, rank),
+        ],
+        2 * (group - 1) + wide - 1, 2, (unfold_three,),
+    )
+    core = core.reshape(rank // group, rank, rank).transpose(1, 0, 2).reshape(rank, shares)
+    return basis_one, basis_two, basis_three, core
 
 
 def orthonormal(basis, gram):
@@ -24,7 +305,7 @@
     return whole.reshape(partial_value.shape)
 
 
-def on_device(window_data, factor_one, factor_two, factor_three):
+def plain_on_device(window_data, factor_one, factor_two, factor_three):
     rank = factor_one.shape[1]
     along_two = contract("kij,jb->kib", window_data, factor_two)
     unfold_part = contract("kib,kc->ibc", along_two, factor_three).reshape(
@@ -53,9 +334,26 @@
     return (basis_one, basis_two, basis_three, core_shares)
 
 
+def program(wide, narrow, window_data, factor_one, factor_two, factor_three):
+    layers, rows, cells = window_data.shape
+    rank = factor_one.shape[1]
+    group = wide * narrow
+    even = (
+        narrow == 2
+        and rank % (8 * narrow) == 0
+        and rank % group == 0
+        and (rank // wide * rows) % 128 == 0
+        and rows % (8 * wide) == 0
+        and cells % (8 * group) == 0
+        and layers % 8 == 0
+    )
+    body = functools.partial(on_device, wide, narrow) if even else plain_on_device
+    return body(window_data, factor_one, factor_two, factor_three)
+
+
 def solution(mesh):
     return jax.shard_map(
-        on_device,
+        functools.partial(program, mesh.shape["wide"], mesh.shape["narrow"]),
         mesh=mesh,
         in_specs=(
             P(("win", "wide"), "narrow", None),

time: 506 us -> 118 us (0.23)
  waiting for transfers between devices: 234 us -> 0 us
  blocking collectives: 180 us -> 0 us
  Pallas kernels: 0 us -> 91.9 us
  other arithmetic: 28.2 us -> 0.12 us
  matrix products: 30.3 us -> 15.4 us
  between operations: 14.1 us -> 0.77 us
  local copies, waits for them, and re-layouts: 18.5 us -> 9.98 us
    unnamed x7 -> x0, waiting for transfers between devices: 166 us -> none
    psum x6 -> x0, blocking collectives: 136 us -> none  [the longest x1 57.9 us: on_device(): lax.psum(contract('kaj,kab->jb', along_one, spread_two), ('wide', 'narrow'))]
    pallas_call x0 -> x3, Pallas kernels: none -> 91.9 us  [call(): pl.pallas_call(functools.partial(kernel, wide, narrow), out_shape=[jax.Sh...]
    reduce_scatter x1 -> x0, waiting for transfers between devices: 67.2 us -> none  [on_device(): lax.psum_scatter(unfold_part, 'wide', scatter_dimension=1, tiled=True)]
    all_gather x2 -> x0, blocking collectives: 43.6 us -> none  [full_core(): whole = lax.all_gather(shares, ('wide', 'narrow'), axis=1, tiled=True)]
    another operation x15 -> x0, other arithmetic: 28.2 us -> none  [the longest x9 15.2 us: orthonormal(): lower = jnp.linalg.cholesky(gram)]
    dot_general x12 -> x7, matrix products: 26.7 us -> 15.4 us  [contract(): return jnp.einsum(form, left, right, precision=highest)]
    unnamed x24 -> x11, local copies, waits for them, and re-layouts: 12.9 us -> 3.64 us
  transfers between devices with their start and end apart: 4 -> 0, of which waited for: 4 -> 0; matrix products, arithmetic and copies ran while one was open for 0% -> 0% of each run, Pallas kernels for 0% -> 0%
where the time goes in v1:
time: 118 us
  Pallas kernels  91.9 us (78%)
  matrix products  15.4 us (13%)
  local copies, waits for them, and re-layouts  9.98 us (8%)
    pallas_call x3, Pallas kernels, call(): pl.pallas_call(functools.partial(kernel, wide, narrow), out_shape=[jax.Sh...  91.9 us
    dot_general x7, matrix products, contract(): return jnp.einsum(form, left, right, precision=highest)  15.4 us
    unnamed x11, local copies, waits for them, and re-layouts  3.64 us
    dot_general x1, local copies, waits for them, and re-layouts, contract(): return jnp.einsum(form, left, right, precision=highest)  2.4 us

profile of v1, /device:TPU:0, one launch (start us, length us, event | category | flops | bytes accessed | tf_op | source)
XLA Modules:
  0.0 118.2 jit_solution(11930426611814486871)
XLA Ops:
  0.6 0.9 copy.17.f_ref
  1.6 1.4 %broadcast_in_dim.2 = f32[24,16,48]{2,0,1:T(8,128)} broadcast(f32[24,48]{1,0:T(8,128)} %param.7), dimensions={0,2} | broadcast | bytes 78336 | tf_op jit(solution)/shard_map/broadcast_in_dim | solution.py:279
  3.0 3.1 %convolution_bitcast_fusion.3 = f32[24,48,64]{2,1,0:T(8,128)S(1)} fusion(f32[24,64,256]{2,1,0:T(8,128)S(1)} %copy-done, f32[256,48]{0,1:T(8,128)} %param.6), kind=kOutput, calls=%fused_computation.5 | convolution fusion | flops 226492416 | bytes 1916928 | tf_op jit(solution)/shard_map/kij,jb->kbi/dot_general | solution.py:15
  6.1 0.2 reshape.29
  6.3 0.7 convolution_bitcast_fusion.u_ref
  7.0 43.6 %shard_map.75 = (f32[64,48]{1,0:T(8,128)S(1)}, f32[8,48,288]{2,1,0:T(8,128)S(1)}) custom-call(f32[48,3072]{1,0:T(8,128)S(1)} %convolution_bitcast_fusion.u_ref, f32[64,48]{1,0:T(8,128)S(1)} %copy.17.f_ref), custom_call_target="tpu_custom_call" | custom-call | tf_op jit(solution)/shard_map/pallas_call | solution.py:232
  50.6 0.7 copy.26
  51.3 1.6 %reshape.30 = f32[8,48,6,48]{3,2,1,0:T(8,128)} reshape(f32[8,48,288]{2,1,0:T(8,128)S(1)} %get-tuple-element.9) | data formatting | bytes 884736 | tf_op jit(solution)/shard_map/reshape | solution.py:264
  52.9 2.2 %fusion.2 = f32[8,6,48,24]{2,3,1,0:T(8,128)S(1)} fusion(f32[8,48,6,48]{3,2,1,0:T(8,128)} %reshape.30, f32[24,48]{1,0:T(8,128)S(1)} %copy-done.2), kind=kOutput, calls=%fused_computation.6 | convolution fusion | flops 31850496 | bytes 668160 | tf_op jit(solution)/shard_map/wcva,kc->kawv/dot_general | solution.py:15
  55.2 0.2 copy.22
  55.4 1.2 %convolution_bitcast_fusion.1 = f32[256,48,24]{0,1,2:T(8,128)S(1)} fusion(f32[24,64,256]{2,1,0:T(8,128)S(1)} %copy-done, f32[64,48]{1,0:T(8,128)S(1)} %get-tuple-element.16), kind=kOutput, calls=%fused_computation.3 | convolution fusion | flops 226492416 | bytes 2764800 | tf_op jit(solution)/shard_map/kij,ia->kaj/dot_general | solution.py:15
  56.7 2.4 %copy.19 = f32[256,48,24]{1,2,0:T(8,128)} copy(f32[256,48,24]{0,1,2:T(8,128)S(1)} %convolution_bitcast_fusion.1) | data formatting | bytes 2359296 | tf_op jit(solution)/shard_map/kaj,kab->jb/dot_general | solution.py:15
  59.1 4.8 %fusion.4.p_ref = f32[16,16,48]{2,1,0:T(8,128)S(1)} fusion(f32[16,16,48,24]{2,3,1,0:T(8,128)} %bitcast.48, f32[24,48,48]{2,1,0:T(8,128)S(1)} %copy.22), kind=kOutput, calls=%fused_computation.8 | convolution fusion | flops 169869312 | bytes 1449984 | tf_op jit(solution)/shard_map/kaj,kab->jb/dot_general | solution.py:15
  63.9 20.0 %shard_map.76 = f32[256,48]{1,0:T(8,128)S(1)} custom-call(f32[16,16,48]{2,1,0:T(8,128)S(1)} %fusion.4.p_ref), custom_call_target="tpu_custom_call" | custom-call | tf_op jit(solution)/shard_map/pallas_call | solution.py:232
  83.9 0.7 copy.27
  84.6 2.6 %convolution_bitcast_fusion.2 = f32[24,64,48]{1,2,0:T(8,128)S(1)} fusion(f32[24,64,256]{2,1,0:T(8,128)S(1)} %copy-done, f32[256,48]{1,0:T(8,128)S(1)} %shard_map.76), kind=kOutput, calls=%fused_computation.4 | convolution fusion | flops 226492416 | bytes 1916928 | tf_op jit(solution)/shard_map/kij,jb->kib/dot_general | solution.py:15
  87.3 0.6 fusion.10
  87.9 0.2 reshape.32
  88.1 0.2 copy.24
  88.3 0.1 maximum_bitcast_fusion.u_ref
  88.4 28.3 %shard_map.77 = (f32[24,48]{1,0:T(8,128)S(1)}, f32[144,48]{1,0:T(8,128)S(1)}) custom-call(f32[16,24,192]{2,1,0:T(8,128)S(1)} %maximum_bitcast_fusion.u_ref), custom_call_target="tpu_custom_call" | custom-call | tf_op jit(solution)/shard_map/pallas_call | solution.py:232
  116.8 0.1 copy.25
  116.8 0.7 copy.28
  117.6 0.6 copy.42
  (6 shorter events, 0.0 us)
Async XLA Ops:
  0.6 2.3 %copy-start = (f32[24,64,256]{2,1,0:T(8,128)S(1)}, f32[24,64,256]{2,1,0:T(8,128)}, u32[]{:S(2)}) copy-start(f32[24,64,256]{2,1,0:T(8,128)} %param.4) | copy-start | bytes 4718596
  3.0 3.3 %copy-start.2 = (f32[24,48]{1,0:T(8,128)S(1)}, f32[24,48]{1,0:T(8,128)}, u32[]{:S(2)}) copy-start(f32[24,48]{1,0:T(8,128)} %param.7) | copy-start | bytes 13828
  87.3 1.0 copy-start.1

commit v2 on v1

--- a/solution.py
+++ b/solution.py
@@ -13,6 +13,10 @@
 
 def contract(form, left, right):
     return jnp.einsum(form, left, right, precision=highest)
+
+
+def contract_high(form, left, right):
+    return jnp.einsum(form, left, right, precision=lax.Precision.HIGH)
 
 
 def dot(left, right):
@@ -248,8 +252,8 @@
     group = wide * narrow
     per = rank // wide
     share = per * rows
-    along_two = contract("kij,jb->kbi", window_data, factor_two).reshape(layers, rank * rows)
-    unfold_one = contract("kc,kn->cn", factor_three, along_two)
+    along_two = contract_high("kij,jb->kbi", window_data, factor_two).reshape(layers, rank * rows)
+    unfold_one = contract_high("kc,kn->cn", factor_three, along_two)
     basis_one, core_two = call(
         mode_one_kernel, wide, narrow,
         [(rows, rank), (wide, rank, per * rank)],
@@ -262,17 +266,17 @@
         4 * (wide - 1) + 3 + group - 1, 0, (unfold_one, factor_one),
     )
     core_two = core_two.reshape(wide, rank, per, rank)
-    along_one = contract("kij,ia->kaj", window_data, basis_one)
-    spread_two = contract("wcva,kc->kawv", core_two, factor_three).reshape(layers, rank, rank)
-    product_two = contract("kaj,kab->jb", along_one, spread_two)
+    along_one = contract_high("kij,ia->kaj", window_data, basis_one)
+    spread_two = contract_high("wcva,kc->kawv", core_two, factor_three).reshape(layers, rank, rank)
+    product_two = contract_high("kaj,kab->jb", along_one, spread_two)
     basis_two, = call(
         mode_two_kernel, wide, narrow,
         [(cells, rank)],
         [(group - 1, cells // group, rank), (group, cells // group, rank)],
         2 * (group - 1), 1, (product_two.reshape(group, cells // group, rank),),
     )
-    along_new = contract("kij,jb->kib", window_data, basis_two)
-    unfold_three = contract("kib,ia->kba", along_new, basis_one)
+    along_new = contract_high("kij,jb->kib", window_data, basis_two)
+    unfold_three = contract_high("kib,ia->kba", along_new, basis_one)
     shares = rank // group * rank
     unfold_three = unfold_three.reshape(layers, group, shares)
     unfold_three = jnp.concatenate(

time: 118 us -> 114 us (0.966)
  matrix products: 15.4 us -> 10.5 us
    dot_general x7, matrix products: 15.4 us -> 10.5 us  [contract_high(): return jnp.einsum(form, left, right, precision=lax.Precision.HIGH)]
where the time goes in v2:
time: 114 us; the launch traced here: 113 us
  Pallas kernels  91.9 us (81%)
  matrix products  10.5 us (9%)
  local copies, waits for them, and re-layouts  10.1 us (9%)
    pallas_call x3, Pallas kernels, call(): pl.pallas_call(functools.partial(kernel, wide, narrow), out_shape=[jax.Sh...  91.9 us
    dot_general x7, matrix products, contract_high(): return jnp.einsum(form, left, right, precision=lax.Precision.HIGH)  10.5 us
    unnamed x11, local copies, waits for them, and re-layouts  3.75 us
    dot_general x1, local copies, waits for them, and re-layouts, contract_high(): return jnp.einsum(form, left, right, precision=lax.Precision.HIGH)  2.4 us

profile of v2, /device:TPU:0, one launch (start us, length us, event | category | flops | bytes accessed | tf_op | source)
XLA Modules:
  0.0 113.4 jit_solution(7567563005696949957)
XLA Ops:
  0.6 0.9 copy.17.f_ref
  1.6 1.4 %broadcast_in_dim.2 = f32[24,16,48]{2,0,1:T(8,128)} broadcast(f32[24,48]{1,0:T(8,128)} %param.7), dimensions={0,2} | broadcast | bytes 78336 | tf_op jit(solution)/shard_map/broadcast_in_dim | solution.py:283
  3.0 2.0 %convolution_bitcast_fusion.3 = f32[24,48,64]{2,1,0:T(8,128)S(1)} fusion(f32[24,64,256]{2,1,0:T(8,128)S(1)} %copy-done, f32[256,48]{0,1:T(8,128)} %param.6), kind=kOutput, calls=%fused_computation.5 | convolution fusion | flops 113246208 | bytes 1916928 | tf_op jit(solution)/shard_map/kij,jb->kbi/dot_general | solution.py:19
  5.0 0.2 reshape.29
  5.2 0.4 convolution_bitcast_fusion.u_ref
  5.7 43.6 %shard_map.75 = (f32[64,48]{1,0:T(8,128)S(1)}, f32[8,48,288]{2,1,0:T(8,128)S(1)}) custom-call(f32[48,3072]{1,0:T(8,128)S(1)} %convolution_bitcast_fusion.u_ref, f32[64,48]{1,0:T(8,128)S(1)} %copy.17.f_ref), custom_call_target="tpu_custom_call" | custom-call | tf_op jit(solution)/shard_map/pallas_call | solution.py:236
  49.3 0.7 copy.26
  50.0 1.6 %reshape.30 = f32[8,48,6,48]{3,2,1,0:T(8,128)} reshape(f32[8,48,288]{2,1,0:T(8,128)S(1)} %get-tuple-element.9) | data formatting | bytes 884736 | tf_op jit(solution)/shard_map/reshape | solution.py:268
  51.6 1.9 %fusion.2 = f32[8,6,48,24]{2,3,1,0:T(8,128)S(1)} fusion(f32[8,48,6,48]{3,2,1,0:T(8,128)} %reshape.30, f32[24,48]{1,0:T(8,128)S(1)} %copy-done.2), kind=kOutput, calls=%fused_computation.6 | convolution fusion | flops 15925248 | bytes 668160 | tf_op jit(solution)/shard_map/wcva,kc->kawv/dot_general | solution.py:19
  53.5 0.2 copy.22
  53.8 0.7 convolution_bitcast_fusion.1
  54.4 2.4 %copy.19 = f32[256,48,24]{1,2,0:T(8,128)} copy(f32[256,48,24]{0,1,2:T(8,128)S(1)} %convolution_bitcast_fusion.1) | data formatting | bytes 2359296 | tf_op jit(solution)/shard_map/kaj,kab->jb/dot_general | solution.py:19
  56.8 3.6 %fusion.4.p_ref = f32[16,16,48]{2,1,0:T(8,128)S(1)} fusion(f32[16,16,48,24]{2,3,1,0:T(8,128)} %bitcast.48, f32[24,48,48]{2,1,0:T(8,128)S(1)} %copy.22), kind=kOutput, calls=%fused_computation.8 | convolution fusion | flops 84934656 | bytes 1449984 | tf_op jit(solution)/shard_map/kaj,kab->jb/dot_general | solution.py:19
  60.5 20.0 %shard_map.76 = f32[256,48]{1,0:T(8,128)S(1)} custom-call(f32[16,16,48]{2,1,0:T(8,128)S(1)} %fusion.4.p_ref), custom_call_target="tpu_custom_call" | custom-call | tf_op jit(solution)/shard_map/pallas_call | solution.py:236
  80.5 0.7 copy.27
  81.2 1.4 %convolution_bitcast_fusion.2 = f32[24,64,48]{1,2,0:T(8,128)S(1)} fusion(f32[24,64,256]{2,1,0:T(8,128)S(1)} %copy-done, f32[256,48]{1,0:T(8,128)S(1)} %shard_map.76), kind=kOutput, calls=%fused_computation.4 | convolution fusion | flops 113246208 | bytes 1916928 | tf_op jit(solution)/shard_map/kij,jb->kib/dot_general | solution.py:19
  82.6 0.4 fusion.10
  83.0 0.2 reshape.32
  83.2 0.2 copy.24
  83.4 0.1 copy-done.1
  83.5 0.1 maximum_bitcast_fusion.u_ref
  83.7 28.3 %shard_map.77 = (f32[24,48]{1,0:T(8,128)S(1)}, f32[144,48]{1,0:T(8,128)S(1)}) custom-call(f32[16,24,192]{2,1,0:T(8,128)S(1)} %maximum_bitcast_fusion.u_ref), custom_call_target="tpu_custom_call" | custom-call | tf_op jit(solution)/shard_map/pallas_call | solution.py:236
  112.1 0.7 copy.28
  112.8 0.6 copy.42
  (6 shorter events, 0.1 us)
Async XLA Ops:
  0.6 2.3 %copy-start = (f32[24,64,256]{2,1,0:T(8,128)S(1)}, f32[24,64,256]{2,1,0:T(8,128)}, u32[]{:S(2)}) copy-start(f32[24,64,256]{2,1,0:T(8,128)} %param.4) | copy-start | bytes 4718596
  3.0 2.2 %copy-start.2 = (f32[24,48]{1,0:T(8,128)S(1)}, f32[24,48]{1,0:T(8,128)}, u32[]{:S(2)}) copy-start(f32[24,48]{1,0:T(8,128)} %param.7) | copy-start | bytes 13828
  82.6 0.9 copy-start.1

commit v3 on v2

--- a/solution.py
+++ b/solution.py
@@ -266,9 +266,9 @@
         4 * (wide - 1) + 3 + group - 1, 0, (unfold_one, factor_one),
     )
     core_two = core_two.reshape(wide, rank, per, rank)
-    along_one = contract_high("kij,ia->kaj", window_data, basis_one)
-    spread_two = contract_high("wcva,kc->kawv", core_two, factor_three).reshape(layers, rank, rank)
-    product_two = contract_high("kaj,kab->jb", along_one, spread_two)
+    along_one = contract_high("kij,ia->akj", window_data, basis_one)
+    spread_two = contract_high("wcva,kc->akwv", core_two, factor_three).reshape(rank, layers, rank)
+    product_two = contract_high("akj,akb->jb", along_one, spread_two)
     basis_two, = call(
         mode_two_kernel, wide, narrow,
         [(cells, rank)],

time: 114 us -> 114 us (level)
  no operation moved by 1% of the time
where the time goes in v3:
time: 114 us; the launch traced here: 113 us
  Pallas kernels  91.9 us (81%)
  matrix products  10.5 us (9%)
  local copies, waits for them, and re-layouts  10.1 us (9%)
    pallas_call x3, Pallas kernels, call(): pl.pallas_call(functools.partial(kernel, wide, narrow), out_shape=[jax.Sh...  91.9 us
    dot_general x7, matrix products, contract_high(): return jnp.einsum(form, left, right, precision=lax.Precision.HIGH)  10.5 us
    unnamed x11, local copies, waits for them, and re-layouts  3.75 us
    dot_general x1, local copies, waits for them, and re-layouts, contract_high(): return jnp.einsum(form, left, right, precision=lax.Precision.HIGH)  2.4 us

profile of v3, /device:TPU:0, one launch (start us, length us, event | category | flops | bytes accessed | tf_op | source)
XLA Modules:
  0.0 113.4 jit_solution(7567563005696949957)
XLA Ops:
  0.6 0.9 copy.17.f_ref
  1.6 1.4 %broadcast_in_dim.2 = f32[24,16,48]{2,0,1:T(8,128)} broadcast(f32[24,48]{1,0:T(8,128)} %param.7), dimensions={0,2} | broadcast | bytes 78336 | tf_op jit(solution)/shard_map/broadcast_in_dim | solution.py:283
  3.0 2.0 %convolution_bitcast_fusion.3 = f32[24,48,64]{2,1,0:T(8,128)S(1)} fusion(f32[24,64,256]{2,1,0:T(8,128)S(1)} %copy-done, f32[256,48]{0,1:T(8,128)} %param.6), kind=kOutput, calls=%fused_computation.5 | convolution fusion | flops 113246208 | bytes 1916928 | tf_op jit(solution)/shard_map/kij,jb->kbi/dot_general | solution.py:19
  5.0 0.2 reshape.29
  5.2 0.4 convolution_bitcast_fusion.u_ref
  5.7 43.6 %shard_map.75 = (f32[64,48]{1,0:T(8,128)S(1)}, f32[8,48,288]{2,1,0:T(8,128)S(1)}) custom-call(f32[48,3072]{1,0:T(8,128)S(1)} %convolution_bitcast_fusion.u_ref, f32[64,48]{1,0:T(8,128)S(1)} %copy.17.f_ref), custom_call_target="tpu_custom_call" | custom-call | tf_op jit(solution)/shard_map/pallas_call | solution.py:236
  49.3 0.7 copy.26
  50.0 1.6 %reshape.30 = f32[8,48,6,48]{3,2,1,0:T(8,128)} reshape(f32[8,48,288]{2,1,0:T(8,128)S(1)} %get-tuple-element.9) | data formatting | bytes 884736 | tf_op jit(solution)/shard_map/reshape | solution.py:268
  51.6 1.9 %fusion.2 = f32[8,6,48,24]{2,3,1,0:T(8,128)S(1)} fusion(f32[8,48,6,48]{3,2,1,0:T(8,128)} %reshape.30, f32[24,48]{1,0:T(8,128)S(1)} %copy-done.2), kind=kOutput, calls=%fused_computation.6 | convolution fusion | flops 15925248 | bytes 668160 | tf_op jit(solution)/shard_map/wcva,kc->akwv/dot_general | solution.py:19
  53.5 0.2 copy.22
  53.8 0.7 convolution_bitcast_fusion.1
  54.4 2.4 %copy.19 = f32[256,48,24]{1,2,0:T(8,128)} copy(f32[256,48,24]{0,1,2:T(8,128)S(1)} %convolution_bitcast_fusion.1) | data formatting | bytes 2359296 | tf_op jit(solution)/shard_map/akj,akb->jb/dot_general | solution.py:19
  56.8 3.6 %fusion.4.p_ref = f32[16,16,48]{2,1,0:T(8,128)S(1)} fusion(f32[16,16,48,24]{2,3,1,0:T(8,128)} %bitcast.48, f32[48,24,48]{2,0,1:T(8,128)S(1)} %copy.22), kind=kOutput, calls=%fused_computation.8 | convolution fusion | flops 84934656 | bytes 1449984 | tf_op jit(solution)/shard_map/akj,akb->jb/dot_general | solution.py:19
  60.5 20.0 %shard_map.76 = f32[256,48]{1,0:T(8,128)S(1)} custom-call(f32[16,16,48]{2,1,0:T(8,128)S(1)} %fusion.4.p_ref), custom_call_target="tpu_custom_call" | custom-call | tf_op jit(solution)/shard_map/pallas_call | solution.py:236
  80.5 0.7 copy.27
  81.2 1.4 %convolution_bitcast_fusion.2 = f32[24,64,48]{1,2,0:T(8,128)S(1)} fusion(f32[24,64,256]{2,1,0:T(8,128)S(1)} %copy-done, f32[256,48]{1,0:T(8,128)S(1)} %shard_map.76), kind=kOutput, calls=%fused_computation.4 | convolution fusion | flops 113246208 | bytes 1916928 | tf_op jit(solution)/shard_map/kij,jb->kib/dot_general | solution.py:19
  82.6 0.4 fusion.10
  83.0 0.2 reshape.32
  83.2 0.2 copy.24
  83.4 0.1 copy-done.1
  83.5 0.1 maximum_bitcast_fusion.u_ref
  83.7 28.3 %shard_map.77 = (f32[24,48]{1,0:T(8,128)S(1)}, f32[144,48]{1,0:T(8,128)S(1)}) custom-call(f32[16,24,192]{2,1,0:T(8,128)S(1)} %maximum_bitcast_fusion.u_ref), custom_call_target="tpu_custom_call" | custom-call | tf_op jit(solution)/shard_map/pallas_call | solution.py:236
  112.1 0.7 copy.28
  112.8 0.6 copy.42
  (6 shorter events, 0.1 us)
Async XLA Ops:
  0.6 2.3 %copy-start = (f32[24,64,256]{2,1,0:T(8,128)S(1)}, f32[24,64,256]{2,1,0:T(8,128)}, u32[]{:S(2)}) copy-start(f32[24,64,256]{2,1,0:T(8,128)} %param.4) | copy-start | bytes 4718596
  3.0 2.2 %copy-start.2 = (f32[24,48]{1,0:T(8,128)S(1)}, f32[24,48]{1,0:T(8,128)}, u32[]{:S(2)}) copy-start(f32[24,48]{1,0:T(8,128)} %param.7) | copy-start | bytes 13828
  82.6 0.9 copy-start.1

commit v4 on v2

--- a/solution.py
+++ b/solution.py
@@ -43,20 +43,18 @@
     both = jnp.concatenate([gram, (rows == columns).astype(jnp.float32)], axis=1)
     blocks = [both[at : at + group] for at in range(0, rank, group)]
     inside = lax.broadcasted_iota(jnp.int32, (group, 2 * rank), 0)
-    scales = []
+    pivots = [jnp.ones((group, 2 * rank), jnp.float32) for _ in blocks]
     for step in range(rank):
         at, row = divmod(step, group)
-        pivot_row = blocks[at][row : row + 1]
-        pivot = pivot_row[:, step : step + 1]
-        scales.append(lax.rsqrt(pivot))
-        scaled = pivot_row * (1.0 / pivot)
-        for later in range(at, rank // group):
-            change = blocks[later][:, step : step + 1] * scaled
-            if later == at:
-                change = jnp.where(inside > row, change, 0.0)
-            blocks[later] = blocks[later] - change
-    right = jnp.concatenate(blocks, axis=0)[:, rank:]
-    return right * jnp.concatenate(scales, axis=0)
+        column = jnp.broadcast_to(blocks[at][:, step : step + 1], (group, 2 * rank))
+        pivot = column[row : row + 1]
+        pivots[at] = jnp.where(inside == row, pivot, pivots[at])
+        scaled = blocks[at][row : row + 1] * (1.0 / pivot)
+        blocks[at] = blocks[at] - jnp.where(inside > row, column * scaled, 0.0)
+        for later in range(at + 1, rank // group):
+            blocks[later] = blocks[later] - blocks[later][:, step : step + 1] * scaled
+    blocks = [block * lax.rsqrt(pivot) for block, pivot in zip(blocks, pivots)]
+    return jnp.concatenate(blocks, axis=0)[:, rank:]
 
 
 class Link:
@@ -103,7 +101,7 @@
             copy.wait_send()
 
 
-def mode_one_kernel(wide, narrow, u_ref, f_ref, basis_ref, core_ref,
+def mode_one_kernel(wide, narrow, u_ref, f_ref, basis_ref, dual_ref, core_ref,
                     parts, total, w_send, w_recv, p_send, p_recv, p_all, c_part, c_recv, c_all, send, recv):
     link = Link(wide, narrow, send, recv)
     share = total.shape[1]
@@ -144,11 +142,9 @@
     for copy in copies:
         copy.wait_recv()
     whole = p_all[...].reshape(narrow * rows, rank)
-    inverse = inverse_lower(dot_t(whole, whole))
-    basis = dot_rt(p_all[pl.ds(link.n * wide, wide)].reshape(rows, rank), inverse)
-    basis_ref[...] = basis
+    held = p_all[pl.ds(link.n * wide, wide)].reshape(rows, rank)
     for v in range(per):
-        c_part[:, v * rank : (v + 1) * rank] = dot(total[:, v * rows : (v + 1) * rows], basis)
+        c_part[:, v * rank : (v + 1) * rank] = dot(total[:, v * rows : (v + 1) * rows], held)
     theirs = pl.ds(pl.multiple_of(partner * half, 8), half)
     copy = link.put(c_part.at[theirs, :], c_recv, link.w, partner)
     own = c_part[pl.ds(pl.multiple_of(link.n * half, 8), half), :]
@@ -157,6 +153,10 @@
     block = c_all.at[link.w, link.n]
     copies = [link.put(block, block, w, link.n) for _, w in link.along_wide()]
     passed = [link.put(block, block, link.w, partner)]
+    inverse = inverse_lower(dot_t(whole, whole))
+    basis = dot_rt(held, inverse)
+    basis_ref[...] = basis
+    dual_ref[...] = dot(basis, inverse)
     for (step, _), copy in zip(link.along_wide(), copies):
         copy.wait_recv()
         source = lax.rem(link.w + wide - step, wide)
@@ -254,9 +254,9 @@
     share = per * rows
     along_two = contract_high("kij,jb->kbi", window_data, factor_two).reshape(layers, rank * rows)
     unfold_one = contract_high("kc,kn->cn", factor_three, along_two)
-    basis_one, core_two = call(
+    basis_one, dual_one, core_two = call(
         mode_one_kernel, wide, narrow,
-        [(rows, rank), (wide, rank, per * rank)],
+        [(rows, rank), (rows, rank), (wide, rank, per * rank)],
         [
             (wide - 1, rank, share), (rank, share),
             (per, rank, rank), (per, rank, rank),
@@ -266,7 +266,7 @@
         4 * (wide - 1) + 3 + group - 1, 0, (unfold_one, factor_one),
     )
     core_two = core_two.reshape(wide, rank, per, rank)
-    along_one = contract_high("kij,ia->kaj", window_data, basis_one)
+    along_one = contract_high("kij,ia->kaj", window_data, dual_one)
     spread_two = contract_high("wcva,kc->kawv", core_two, factor_three).reshape(layers, rank, rank)
     product_two = contract_high("kaj,kab->jb", along_one, spread_two)
     basis_two, = call(

time: 114 us -> 114 us (level)
    unnamed x11 -> x13, local copies, waits for them, and re-layouts: 3.75 us -> 3.76 us
where the time goes in v4:
time: 114 us
  Pallas kernels  91.7 us (80%)
  local copies, waits for them, and re-layouts  10.7 us (9%)
  matrix products  10.5 us (9%)
    pallas_call x3, Pallas kernels, call(): pl.pallas_call(functools.partial(kernel, wide, narrow), out_shape=[jax.Sh...  91.7 us
    dot_general x7, matrix products, contract_high(): return jnp.einsum(form, left, right, precision=lax.Precision.HIGH)  10.5 us
    unnamed x13, local copies, waits for them, and re-layouts  3.76 us

profile of v4, /device:TPU:0, one launch (start us, length us, event | category | flops | bytes accessed | tf_op | source)
XLA Modules:
  0.0 113.8 jit_solution(6537176206787705735)
XLA Ops:
  0.6 0.9 copy.17.f_ref
  1.6 1.4 %broadcast_in_dim.2 = f32[24,16,48]{2,0,1:T(8,128)} broadcast(f32[24,48]{1,0:T(8,128)} %param.7), dimensions={0,2} | broadcast | bytes 78336 | tf_op jit(solution)/shard_map/broadcast_in_dim | solution.py:283
  3.0 2.0 %convolution_bitcast_fusion.3 = f32[24,48,64]{2,1,0:T(8,128)S(1)} fusion(f32[24,64,256]{2,1,0:T(8,128)S(1)} %copy-done, f32[256,48]{0,1:T(8,128)} %param.6), kind=kOutput, calls=%fused_computation.5 | convolution fusion | flops 113246208 | bytes 1916928 | tf_op jit(solution)/shard_map/kij,jb->kbi/dot_general | solution.py:19
  5.0 0.2 reshape.29
  5.2 0.4 convolution_bitcast_fusion.u_ref
  5.6 43.5 %shard_map.75 = (f32[64,48]{1,0:T(8,128)S(1)}, f32[64,48]{1,0:T(8,128)S(1)}, f32[8,48,288]{2,1,0:T(8,128)S(1)}) custom-call(f32[48,3072]{1,0:T(8,128)S(1)} %convolution_bitcast_fusion.u_ref, f32[64,48]{1,0:T(8,128)S(1)} %copy.17.f_ref), custom_call_target="tpu_custom_call" | custom-call | tf_op jit(solution)/shard_map/pallas_call | solution.py:236
  49.1 0.7 copy.26
  49.8 0.7 convolution_bitcast_fusion.1
  50.5 1.6 %reshape.30 = f32[8,48,6,48]{3,2,1,0:T(8,128)} reshape(f32[8,48,288]{2,1,0:T(8,128)S(1)} %get-tuple-element.11) | data formatting | bytes 884736 | tf_op jit(solution)/shard_map/reshape | solution.py:268
  52.2 1.9 %fusion.2 = f32[8,6,48,24]{2,3,1,0:T(8,128)S(1)} fusion(f32[8,48,6,48]{3,2,1,0:T(8,128)} %reshape.30, f32[24,48]{1,0:T(8,128)S(1)} %copy-done.3), kind=kOutput, calls=%fused_computation.6 | convolution fusion | flops 15925248 | bytes 668160 | tf_op jit(solution)/shard_map/wcva,kc->kawv/dot_general | solution.py:19
  54.1 1.0 copy.22
  55.1 2.2 %copy.19 = f32[256,48,24]{1,2,0:T(8,128)} copy(f32[256,48,24]{0,1,2:T(8,128)S(1)} %convolution_bitcast_fusion.1) | data formatting | bytes 2359296 | tf_op jit(solution)/shard_map/kaj,kab->jb/dot_general | solution.py:19
  57.4 3.6 %fusion.4.p_ref = f32[16,16,48]{2,1,0:T(8,128)S(1)} fusion(f32[16,16,48,24]{2,3,1,0:T(8,128)} %bitcast.48, f32[24,48,48]{2,1,0:T(8,128)S(1)} %copy-done.1), kind=kOutput, calls=%fused_computation.8 | convolution fusion | flops 84934656 | bytes 1449984 | tf_op jit(solution)/shard_map/kaj,kab->jb/dot_general | solution.py:19
  61.0 20.0 %shard_map.76 = f32[256,48]{1,0:T(8,128)S(1)} custom-call(f32[16,16,48]{2,1,0:T(8,128)S(1)} %fusion.4.p_ref), custom_call_target="tpu_custom_call" | custom-call | tf_op jit(solution)/shard_map/pallas_call | solution.py:236
  81.0 0.7 copy.27
  81.7 1.4 %convolution_bitcast_fusion.2 = f32[24,64,48]{1,2,0:T(8,128)S(1)} fusion(f32[24,64,256]{2,1,0:T(8,128)S(1)} %copy-done, f32[256,48]{1,0:T(8,128)S(1)} %shard_map.76), kind=kOutput, calls=%fused_computation.4 | convolution fusion | flops 113246208 | bytes 1916928 | tf_op jit(solution)/shard_map/kij,jb->kib/dot_general | solution.py:19
  83.1 0.4 fusion.10
  83.5 0.2 reshape.32
  83.7 0.2 copy.24
  83.9 0.1 copy-done.2
  84.0 0.1 maximum_bitcast_fusion.u_ref
  84.1 28.3 %shard_map.77 = (f32[24,48]{1,0:T(8,128)S(1)}, f32[144,48]{1,0:T(8,128)S(1)}) custom-call(f32[16,24,192]{2,1,0:T(8,128)S(1)} %maximum_bitcast_fusion.u_ref), custom_call_target="tpu_custom_call" | custom-call | tf_op jit(solution)/shard_map/pallas_call | solution.py:236
  112.5 0.7 copy.28
  113.2 0.6 copy.42
  (8 shorter events, 0.1 us)
Async XLA Ops:
  0.6 2.3 %copy-start = (f32[24,64,256]{2,1,0:T(8,128)S(1)}, f32[24,64,256]{2,1,0:T(8,128)}, u32[]{:S(2)}) copy-start(f32[24,64,256]{2,1,0:T(8,128)} %param.4) | copy-start | bytes 4718596
  3.0 2.2 %copy-start.3 = (f32[24,48]{1,0:T(8,128)S(1)}, f32[24,48]{1,0:T(8,128)}, u32[]{:S(2)}) copy-start(f32[24,48]{1,0:T(8,128)} %param.7) | copy-start | bytes 13828
  55.1 2.2 %copy-start.1 = (f32[24,48,48]{2,1,0:T(8,128)S(1)}, f32[24,48,48]{2,1,0:T(8,128)}, u32[]{:S(2)}) copy-start(f32[24,48,48]{2,1,0:T(8,128)} %copy.22) | copy-start | bytes 663556
  83.1 0.9 copy-start.2

commit v5 on v2

--- a/solution.py
+++ b/solution.py
@@ -43,20 +43,28 @@
     both = jnp.concatenate([gram, (rows == columns).astype(jnp.float32)], axis=1)
     blocks = [both[at : at + group] for at in range(0, rank, group)]
     inside = lax.broadcasted_iota(jnp.int32, (group, 2 * rank), 0)
-    scales = []
-    for step in range(rank):
-        at, row = divmod(step, group)
-        pivot_row = blocks[at][row : row + 1]
-        pivot = pivot_row[:, step : step + 1]
-        scales.append(lax.rsqrt(pivot))
-        scaled = pivot_row * (1.0 / pivot)
-        for later in range(at, rank // group):
-            change = blocks[later][:, step : step + 1] * scaled
-            if later == at:
-                change = jnp.where(inside > row, change, 0.0)
-            blocks[later] = blocks[later] - change
-    right = jnp.concatenate(blocks, axis=0)[:, rank:]
-    return right * jnp.concatenate(scales, axis=0)
+    wide_shape = (group, 2 * rank)
+    for at in range(rank // group):
+        later = range(at, rank // group)
+        spread = [
+            {k: jnp.broadcast_to(blocks[k][:, at * group + t : at * group + t + 1], wide_shape) for k in later}
+            for t in range(group)
+        ]
+        pivots = jnp.ones(wide_shape, jnp.float32)
+        for row in range(group):
+            pivot = spread[row][at][row : row + 1]
+            pivots = jnp.where(inside == row, pivot, pivots)
+            over = 1.0 / pivot
+            column = dict(spread[row])
+            column[at] = jnp.where(inside > row, column[at], 0.0)
+            for t in range(row + 1, group):
+                factor = spread[t][at][row : row + 1] * over
+                spread[t] = {k: spread[t][k] - column[k] * factor for k in later}
+            scaled = blocks[at][row : row + 1] * over
+            for k in later:
+                blocks[k] = blocks[k] - column[k] * scaled
+        blocks[at] = blocks[at] * lax.rsqrt(pivots)
+    return jnp.concatenate(blocks, axis=0)[:, rank:]
 
 
 class Link:
@@ -265,10 +273,9 @@
         ],
         4 * (wide - 1) + 3 + group - 1, 0, (unfold_one, factor_one),
     )
-    core_two = core_two.reshape(wide, rank, per, rank)
     along_one = contract_high("kij,ia->kaj", window_data, basis_one)
-    spread_two = contract_high("wcva,kc->kawv", core_two, factor_three).reshape(layers, rank, rank)
-    product_two = contract_high("kaj,kab->jb", along_one, spread_two)
+    spread_two = contract_high("wcn,kc->kwn", core_two, factor_three).reshape(layers, rank, rank)
+    product_two = contract_high("kaj,kba->jb", along_one, spread_two)
     basis_two, = call(
         mode_two_kernel, wide, narrow,
         [(cells, rank)],

time: 114 us -> 101 us (0.89)
  Pallas kernels: 91.9 us -> 83.2 us
  local copies, waits for them, and re-layouts: 10.1 us -> 7.67 us
  matrix products: 10.5 us -> 8.89 us
    pallas_call x3, Pallas kernels: 91.9 us -> 83.2 us  [call(): pl.pallas_call(functools.partial(kernel, wide, narrow), out_shape=[jax.Sh...]
    dot_general x7, matrix products: 10.5 us -> 8.89 us  [contract_high(): return jnp.einsum(form, left, right, precision=lax.Precision.HIGH)]
    reshape x2 -> x1, local copies, waits for them, and re-layouts: 1.87 us -> 0.35 us  [on_device(): contract_high('wcn,kc->kwn', core_two, factor_three)]
    broadcast_in_dim x1, local copies, waits for them, and re-layouts: 1.4 us -> 0.01 us  [on_device(): jnp.broadcast_to(factor_three[:, None], (layers, group, rank))]
    dot_general x1 -> x2, local copies, waits for them, and re-layouts: 2.4 us -> 2.46 us  [contract_high(): return jnp.einsum(form, left, right, precision=lax.Precision.HIGH)]
where the time goes in v5:
time: 101 us
  Pallas kernels  83.2 us (82%)
  matrix products  8.89 us (9%)
  local copies, waits for them, and re-layouts  7.67 us (8%)
    pallas_call x3, Pallas kernels, call(): pl.pallas_call(functools.partial(kernel, wide, narrow), out_shape=[jax.Sh...  83.2 us
    dot_general x7, matrix products, contract_high(): return jnp.einsum(form, left, right, precision=lax.Precision.HIGH)  8.89 us
    unnamed x11, local copies, waits for them, and re-layouts  4.17 us
    dot_general x2, local copies, waits for them, and re-layouts, contract_high(): return jnp.einsum(form, left, right, precision=lax.Precision.HIGH)  2.46 us

profile of v5, /device:TPU:0, one launch (start us, length us, event | category | flops | bytes accessed | tf_op | source)
XLA Modules:
  0.0 100.7 jit_solution(5898997741506743877)
XLA Ops:
  0.7 1.4 %copy-done = f32[24,64,256]{2,1,0:T(8,128)S(1)} copy-done((f32[24,64,256]{2,1,0:T(8,128)S(1)}, f32[24,64,256]{2,1,0:T(8,128)}, u32[]{:S(2)}) %copy-start) | copy-done | bytes 1572888
  2.0 2.0 %convolution_bitcast_fusion.3 = f32[24,48,64]{2,1,0:T(8,128)S(1)} fusion(f32[24,64,256]{2,1,0:T(8,128)S(1)} %copy-done, f32[256,48]{0,1:T(8,128)} %param.6), kind=kOutput, calls=%fused_computation.5 | convolution fusion | flops 113246208 | bytes 1916928 | tf_op jit(solution)/shard_map/kij,jb->kbi/dot_general | solution.py:19
  4.1 0.2 reshape.26
  4.3 0.4 convolution_bitcast_fusion.u_ref
  4.7 0.1 copy.15.f_ref
  4.8 40.6 %shard_map.75 = (f32[64,48]{1,0:T(8,128)S(1)}, f32[8,48,288]{2,1,0:T(8,128)S(1)}) custom-call(f32[48,3072]{1,0:T(8,128)S(1)} %convolution_bitcast_fusion.u_ref, f32[64,48]{1,0:T(8,128)S(1)} %copy.15.f_ref), custom_call_target="tpu_custom_call" | custom-call | tf_op jit(solution)/shard_map/pallas_call | solution.py:244
  45.4 0.7 convolution_bitcast_fusion.1
  46.1 2.4 %copy.17 = f32[256,48,24]{1,2,0:T(8,128)} copy(f32[256,48,24]{0,1,2:T(8,128)S(1)} %convolution_bitcast_fusion.1) | data formatting | bytes 2359296 | tf_op jit(solution)/shard_map/kaj,kba->jb/dot_general | solution.py:19
  48.5 0.3 convolution_bitcast_fusion.4
  48.8 0.1 copy.18
  48.9 0.4 reshape.34
  49.2 3.7 %fusion.2.p_ref = f32[16,16,48]{2,1,0:T(8,128)S(1)} fusion(f32[24,48,48,1]{2,1,0,3:T(8,128)S(1)} %reshape.34, f32[16,16,48,24]{2,3,1,0:T(8,128)} %bitcast.44), kind=kOutput, calls=%fused_computation.7 | convolution fusion | flops 84934656 | bytes 1449984 | tf_op jit(solution)/shard_map/kaj,kba->jb/dot_general | solution.py:19
  52.9 17.1 %shard_map.76 = f32[256,48]{1,0:T(8,128)S(1)} custom-call(f32[16,16,48]{2,1,0:T(8,128)S(1)} %fusion.2.p_ref), custom_call_target="tpu_custom_call" | custom-call | tf_op jit(solution)/shard_map/pallas_call | solution.py:244
  70.0 1.4 %convolution_bitcast_fusion.2 = f32[24,64,48]{1,2,0:T(8,128)S(1)} fusion(f32[24,64,256]{2,1,0:T(8,128)S(1)} %copy-done, f32[256,48]{1,0:T(8,128)S(1)} %shard_map.76), kind=kOutput, calls=%fused_computation.4 | convolution fusion | flops 113246208 | bytes 1916928 | tf_op jit(solution)/shard_map/kij,jb->kib/dot_general | solution.py:19
  71.4 0.4 fusion.7
  71.8 0.2 reshape.28
  72.0 0.2 copy.21
  72.2 0.1 maximum_bitcast_fusion.u_ref
  72.4 25.5 %shard_map.77 = (f32[24,48]{1,0:T(8,128)S(1)}, f32[144,48]{1,0:T(8,128)S(1)}) custom-call(f32[16,24,192]{2,1,0:T(8,128)S(1)} %maximum_bitcast_fusion.u_ref), custom_call_target="tpu_custom_call" | custom-call | tf_op jit(solution)/shard_map/pallas_call | solution.py:244
  97.9 0.1 copy.22
  98.0 0.7 copy.25
  98.7 0.7 copy.24
  99.4 0.7 copy.23
  100.1 0.6 copy.36
  (6 shorter events, 0.0 us)
Async XLA Ops:
  0.6 1.4 %copy-start = (f32[24,64,256]{2,1,0:T(8,128)S(1)}, f32[24,64,256]{2,1,0:T(8,128)}, u32[]{:S(2)}) copy-start(f32[24,64,256]{2,1,0:T(8,128)} %param.4) | copy-start | bytes 4718596
  0.6 3.6 %copy-start.1 = (f32[24,48]{1,0:T(8,128)S(1)}, f32[24,48]{1,0:T(8,128)}, u32[]{:S(2)}) copy-start(f32[24,48]{1,0:T(8,128)} %param.7) | copy-start | bytes 13828
  2.0 2.7 %copy-start.2 = (f32[64,48]{0,1:T(8,128)S(1)}, f32[64,48]{0,1:T(8,128)}, u32[]{:S(2)}) copy-start(f32[64,48]{0,1:T(8,128)} %param.5) | copy-start | bytes 36868

commit v6 on v5

--- a/solution.py
+++ b/solution.py
@@ -273,9 +273,9 @@
         ],
         4 * (wide - 1) + 3 + group - 1, 0, (unfold_one, factor_one),
     )
-    along_one = contract_high("kij,ia->kaj", window_data, basis_one)
     spread_two = contract_high("wcn,kc->kwn", core_two, factor_three).reshape(layers, rank, rank)
-    product_two = contract_high("kaj,kba->jb", along_one, spread_two)
+    spread_two = contract_high("kba,ia->kib", spread_two, basis_one)
+    product_two = contract_high("kij,kib->jb", window_data, spread_two)
     basis_two, = call(
         mode_two_kernel, wide, narrow,
         [(cells, rank)],

time: 101 us -> 95.1 us (0.942)
  matrix products: 8.89 us -> 5.53 us
  local copies, waits for them, and re-layouts: 7.67 us -> 5.37 us
    dot_general x7, matrix products: 8.89 us -> 5.53 us  [contract_high(): return jnp.einsum(form, left, right, precision=lax.Precision.HIGH)]
    dot_general x2, local copies, waits for them, and re-layouts: 2.46 us -> 0.15 us  [contract_high(): return jnp.einsum(form, left, right, precision=lax.Precision.HIGH)]
where the time goes in v6:
time: 95.1 us; the launch traced here: 94.9 us
  Pallas kernels  83.1 us (87%)
  matrix products  5.53 us (6%)
  local copies, waits for them, and re-layouts  5.37 us (6%)
    pallas_call x3, Pallas kernels, call(): pl.pallas_call(functools.partial(kernel, wide, narrow), out_shape=[jax.Sh...  83.1 us
    dot_general x7, matrix products, contract_high(): return jnp.einsum(form, left, right, precision=lax.Precision.HIGH)  5.53 us
    unnamed x11, local copies, waits for them, and re-layouts  4.17 us

profile of v6, /device:TPU:0, one launch (start us, length us, event | category | flops | bytes accessed | tf_op | source)
XLA Modules:
  0.0 94.9 jit_solution(13255569162529975379)
XLA Ops:
  0.7 1.4 %copy-done = f32[24,64,256]{2,1,0:T(8,128)S(1)} copy-done((f32[24,64,256]{2,1,0:T(8,128)S(1)}, f32[24,64,256]{2,1,0:T(8,128)}, u32[]{:S(2)}) %copy-start) | copy-done | bytes 1572888
  2.0 2.0 %convolution_bitcast_fusion.3 = f32[24,48,64]{2,1,0:T(8,128)S(1)} fusion(f32[24,64,256]{2,1,0:T(8,128)S(1)} %copy-done, f32[256,48]{0,1:T(8,128)} %param.6), kind=kOutput, calls=%fused_computation.3 | convolution fusion | flops 113246208 | bytes 1916928 | tf_op jit(solution)/shard_map/kij,jb->kbi/dot_general | solution.py:19
  4.1 0.2 reshape.27
  4.3 0.4 convolution_bitcast_fusion.u_ref
  4.7 0.1 copy.14.f_ref
  4.8 40.6 %shard_map.75 = (f32[64,48]{1,0:T(8,128)S(1)}, f32[8,48,288]{2,1,0:T(8,128)S(1)}) custom-call(f32[48,3072]{1,0:T(8,128)S(1)} %convolution_bitcast_fusion.u_ref, f32[64,48]{1,0:T(8,128)S(1)} %copy.14.f_ref), custom_call_target="tpu_custom_call" | custom-call | tf_op jit(solution)/shard_map/pallas_call | solution.py:244
  45.4 0.3 convolution_bitcast_fusion.4
  45.7 0.1 copy.15
  45.8 0.4 reshape.28
  46.2 0.4 convolution_bitcast_fusion.2
  46.6 0.6 convolution_bitcast_fusion.5
  47.1 0.1 copy.16
  47.2 17.1 %shard_map.76 = f32[256,48]{1,0:T(8,128)S(1)} custom-call(f32[16,16,48]{2,1,0:T(8,128)S(1)} %bitcast.45), custom_call_target="tpu_custom_call" | custom-call | tf_op jit(solution)/shard_map/pallas_call | solution.py:244
  64.3 1.4 %convolution_bitcast_fusion.1 = f32[24,64,48]{1,2,0:T(8,128)S(1)} fusion(f32[24,64,256]{2,1,0:T(8,128)S(1)} %copy-done, f32[256,48]{1,0:T(8,128)S(1)} %shard_map.76), kind=kOutput, calls=%fused_computation.1 | convolution fusion | flops 113246208 | bytes 1916928 | tf_op jit(solution)/shard_map/kij,jb->kib/dot_general | solution.py:19
  65.7 0.4 fusion.2
  66.1 0.2 reshape.30
  66.3 0.2 copy.18
  66.6 0.1 maximum_bitcast_fusion.u_ref
  66.7 25.4 %shard_map.77 = (f32[24,48]{1,0:T(8,128)S(1)}, f32[144,48]{1,0:T(8,128)S(1)}) custom-call(f32[16,24,192]{2,1,0:T(8,128)S(1)} %maximum_bitcast_fusion.u_ref), custom_call_target="tpu_custom_call" | custom-call | tf_op jit(solution)/shard_map/pallas_call | solution.py:244
  92.1 0.1 copy.19
  92.2 0.7 copy.22
  92.9 0.7 copy.21
  93.6 0.7 copy.20
  94.3 0.6 copy.26
  (6 shorter events, 0.0 us)
Async XLA Ops:
  0.6 1.4 %copy-start = (f32[24,64,256]{2,1,0:T(8,128)S(1)}, f32[24,64,256]{2,1,0:T(8,128)}, u32[]{:S(2)}) copy-start(f32[24,64,256]{2,1,0:T(8,128)} %param.4) | copy-start | bytes 4718596
  0.6 3.6 %copy-start.1 = (f32[24,48]{1,0:T(8,128)S(1)}, f32[24,48]{1,0:T(8,128)}, u32[]{:S(2)}) copy-start(f32[24,48]{1,0:T(8,128)} %param.7) | copy-start | bytes 13828
  2.0 2.7 %copy-start.2 = (f32[64,48]{0,1:T(8,128)S(1)}, f32[64,48]{0,1:T(8,128)}, u32[]{:S(2)}) copy-start(f32[64,48]{0,1:T(8,128)} %param.5) | copy-start | bytes 36868
